TPU v7x, 128 devices: a whole 4x4x4 slice. The times are simulated.
128 devices in a mesh: dp: 16 (over z_lo, x, core), tensor: 8 (over y, z_hi).
Axes of the slice: x: 4, y: 4, z: 4 (z_hi: 2, z_lo: 2; z = z_hi * 2 + z_lo), core: 2. Of those that a mesh axis runs over, the one named last changes fastest.
Arguments:
- tokens: bfloat16 [1024, 8192], P('tensor', 'dp'), may hold values from -6 to 6
- segment_ids: int32 [1024], replicated, may hold values from 0 to 7, never falling along the last dimension, each value on 1 to 256 neighbouring positions
- gate_weight: bfloat16 [8192, 15360], P('dp', 'tensor'), may hold values from -0.0625 to 0.0625
- up_weight: bfloat16 [8192, 15360], P('dp', 'tensor'), may hold values from -0.0625 to 0.0625
- down_weight: bfloat16 [15360, 8192], P('tensor', 'dp'), may hold values from -0.046875 to 0.046875
- grad_out: bfloat16 [1024, 8192], P('tensor', 'dp'), may hold values from -6 to 6
Outputs:
- mixed: bfloat16 [1024, 8192], P('tensor', 'dp')
- grad_gate: float32 [8192, 15360], P('dp', 'tensor')
- grad_up: float32 [8192, 15360], P('dp', 'tensor')
- grad_down: float32 [15360, 8192], P('tensor', 'dp')
Inputs may be any that keep to these rules, and one draw needn't show every extreme that they name: `segment_ids`: document numbers never fall along the positions; each of the 8 documents has 1 to 256 positions and one has exactly 256.
All inputs are finite; a program needn't handle non-finite values.
Results may differ from a plain program's by a relative error of at most 0.005.
Values may be sent and summed in bfloat16 or wider, within the bound.
A program may use at most 192 MiB of HBM per device.

v0:
```python
import jax
import jax.numpy as jnp
from jax import lax
from jax.experimental import pallas as pl
from jax.experimental.pallas import tpu as pltpu
from jax.sharding import PartitionSpec as P

NSEG = 8
SLOTS = 8
ROWS = 128
HALF = 64
SEG = 16
OWN, MATE = 7, 1
WIDTH = 512
UNITS = 1920
TILE = 128
MESH = pl.DeviceIdType.MESH
BF16 = jnp.bfloat16
F32 = jnp.float32
DOT_COLUMNS = ((0, 512), (512, 512), (1024, 512), (1536, 384))

JOIN = 18
EARLY = 4
EARLY_STEPS = (17, 18)

CA = 1152
CB = UNITS - CA
OA = -(-CA // (2 * TILE)) * TILE
KA = CA - OA
OB = -(-CB // (2 * TILE)) * TILE
KB = CB - OB
OL = OB // (2 * TILE) * TILE
OR = OB - OL

DEPTH = 4
NAMES = (
    "core0", "core1", "core2", "x1p", "x1m", "x2p", "x2m", "zred", "zgat", "g1p", "g1m", "g2p", "g2m", "cgat",
    "mix", "y0", "y1p", "y1m", "y2p", "y2m", "k1p", "k1m", "k2p", "k2m", "k3",
)
KIND = {name: i for i, name in enumerate(NAMES)}


def exchange_kernel(
    ids_hbm, tokens_hbm, grad_out_hbm, wg_hbm, wu_hbm, wd_hbm,
    mown, gat, tokt, hidt, hh, early,
    ids, grad_out, wg, wu, wd, acc, cs, cr, x1s, x1a, x1b, x2s, x2r, zs, zr,
    y0s, y0r, y1s, y1a, y1b, y2s, y2r, ms, mr, mfr, mfar,
    ss, rs, ts, tr, ws, own_sems,
):
    inputs = [
        pltpu.make_async_copy(a, b, own_sems.at[k])
        for k, (a, b) in enumerate(
            ((ids_hbm, ids), (grad_out_hbm, grad_out), (tokens_hbm, gat.at[OWN, :, :WIDTH]))
        )
    ]
    for copy in inputs:
        copy.start()
    weights = [
        pltpu.make_async_copy(a, b, ws.at[k])
        for k, (a, b) in enumerate(((wg_hbm, wg), (wu_hbm, wu), (wd_hbm, wd)))
    ]
    for copy in weights:
        copy.start()

    dp = lax.axis_index("dp")
    tn = lax.axis_index("tensor")
    w, x, q = dp // 8, (dp // 2) % 4, dp % 2
    y, h = tn // 2, tn % 2
    xp, xm, xo = (x + 1) % 4, (x + 3) % 4, (x + 2) % 4

    def dpdev(w=w, x=x, q=q):
        return (w * 8 + x * 2 + q, tn)

    def tdev(dy, dh):
        return (dp, ((y + dy) % 4) * 2 + (h + dh) % 2)

    core, right, left, zmate = dpdev(q=1 - q), dpdev(x=xp), dpdev(x=xm), dpdev(w=1 - w)
    offsets = [(1, 0), (0, 1), (1, 1), (3, 1), (2, 1), (3, 0), (2, 0), (0, 0)]

    barrier = pltpu.get_barrier_semaphore()
    partners = [core, right, left, zmate] + [tdev(*o) for o in offsets[:OWN]]
    for p in partners:
        pl.semaphore_signal(barrier, inc=1, device_id=p, device_id_type=MESH)

    for copy in inputs:
        copy.wait()
    all_ids = ids[...]
    own_ids = ids[pl.ds(tn, 1), :]
    row = jnp.zeros((1, ROWS), F32)
    for s in range(NSEG):
        length = jnp.sum(jnp.where(all_ids == s, 1.0, 0.0), axis=(0, 1), keepdims=True)
        row = jnp.where(own_ids == s, lax.rsqrt(length), row)
    square = jnp.broadcast_to(row, (ROWS, ROWS))
    on_diagonal = lax.broadcasted_iota(jnp.int32, (ROWS, ROWS), 0) == lax.broadcasted_iota(
        jnp.int32, (ROWS, ROWS), 1
    )
    column = jnp.sum(jnp.where(on_diagonal, square, 0.0), axis=1, keepdims=True)
    gat[OWN, :, WIDTH:] = (grad_out[...].astype(F32) * column).astype(BF16)

    pl.semaphore_wait(barrier, len(partners))

    def rows_of(xx):
        return pl.ds(pl.multiple_of(q * HALF + xx * SEG, SEG), SEG)

    def seg_of(xx):
        return pl.ds(pl.multiple_of(xx * SEG, SEG), SEG)

    def half_of(qq):
        return pl.ds(pl.multiple_of(qq * HALF, HALF), HALF)

    def cols_of(start, size):
        return pl.ds(pl.multiple_of(start, TILE), size)

    def msg(name, c, src, dst, dev):
        kind = KIND[name]
        return pltpu.make_async_remote_copy(
            src_ref=src, dst_ref=dst, send_sem=ss.at[kind, c], recv_sem=rs.at[kind, c],
            device_id=dev, device_id_type=MESH,
        )

    def tok_msg(slot, src, dev):
        return pltpu.make_async_remote_copy(
            src_ref=src, dst_ref=gat.at[slot], send_sem=ts.at[slot], recv_sem=tr.at[slot],
            device_id=dev, device_id_type=MESH,
        )

    def in_place(name, c, rows, cols, dev):
        ref = hh.at[c, :, rows, cols]
        return msg(name, c, ref, ref, dev)

    own_a, mate_a = cols_of(w * KA, OA), cols_of((1 - w) * KA, OA)
    out_a, in_a = cols_of(w * OA, KA), cols_of((1 - w) * OA, KA)
    own_b, mate_b = cols_of(CA + w * KB, OB), cols_of(CA + (1 - w) * KB, OB)
    own_b_left = cols_of(CA + w * KB, OL)
    own_b_right = cols_of(CA + w * KB + OL, OR)
    out_b, in_b = cols_of(CA + w * OB, KB), cols_of(CA + (1 - w) * OB, KB)
    all_a, lo_a, hi_a = pl.ds(0, CA), pl.ds(0, OA), pl.ds(OA, KA)

    def m_core(c, k):
        return msg(f"core{k}", c, cs.at[c % 2, k], cr.at[c % 2, k], core)

    def m_x1p(c):
        return msg("x1p", c, x1s.at[c % DEPTH, :, :, lo_a], x1a.at[c % DEPTH], right)

    def m_x1m(c):
        return msg("x1m", c, x1s.at[c % DEPTH, :, :, hi_a], x1b.at[c % DEPTH], left)

    def m_x2p(c):
        return msg("x2p", c, x2s.at[c % DEPTH, 0], x2r.at[c % DEPTH, 0], right)

    def m_x2m(c):
        return msg("x2m", c, x2s.at[c % DEPTH, 1], x2r.at[c % DEPTH, 1], left)

    def m_zred(c):
        return msg("zred", c, zs.at[c % DEPTH], zr.at[c % DEPTH], zmate)

    def m_zgat(c, cols):
        return in_place("zgat", c, rows_of(x), cols, zmate)

    def m_g1p(c, xx):
        return in_place("g1p", c, rows_of(xx), all_a, right)

    def m_g1m(c, xx):
        return in_place("g1m", c, rows_of(xx), all_a, left)

    def m_g2p(c, xx):
        return in_place("g2p", c, rows_of(xx), hi_a, right)

    def m_g2m(c, xx):
        return in_place("g2m", c, rows_of(xx), lo_a, left)

    def m_y0(c):
        return msg("y0", c, y0s.at[c % DEPTH], y0r.at[c % DEPTH], zmate)

    def m_y1p(c):
        return msg("y1p", c, y1s.at[c % DEPTH, :, :, :OL], y1a.at[c % DEPTH], right)

    def m_y1m(c):
        return msg("y1m", c, y1s.at[c % DEPTH, :, :, OL:], y1b.at[c % DEPTH], left)

    def m_y2p(c):
        return msg("y2p", c, y2s.at[c % DEPTH, 0], y2r.at[c % DEPTH, 0], right)

    def m_y2m(c):
        return msg("y2m", c, y2s.at[c % DEPTH, 1], y2r.at[c % DEPTH, 1], left)

    def m_k1p(c, xx):
        return in_place("k1p", c, rows_of(xx), own_b, right)

    def m_k1m(c, xx):
        return in_place("k1m", c, rows_of(xx), own_b, left)

    def m_k2p(c, xx):
        return in_place("k2p", c, rows_of(xx), own_b_right, right)

    def m_k2m(c, xx):
        return in_place("k2m", c, rows_of(xx), own_b_left, left)

    def m_k3(c, cols):
        return in_place("k3", c, half_of(q), cols, zmate)

    def m_cgat(c, qq):
        ref = hh.at[c, :, half_of(qq), :]
        return msg("cgat", c, ref, ref, core)

    def m_mix(c):
        dy = jnp.where(c == 0, 1, jnp.where(c % 2 == 1, 3, jnp.where(c == 2, 1, 2)))
        return msg("mix", c, ms.at[c], mr.at[c], tdev(dy, 0))

    def m_far():
        return msg("mix", OWN, mfar, mfr, tdev(0, 1))

    for s in (0, 5, MATE):
        dy, dh = offsets[s]
        tok_msg(s, gat.at[OWN], tdev(-dy % 4, dh)).start()
    for copy in weights:
        copy.wait()

    def a_partials(c, r):
        @pl.when((c != OWN) & (c != MATE))
        def _():
            tok_msg(c, gat.at[OWN], core).wait_recv()

        both = jnp.concatenate([gat[c, half_of(1 - q), :], gat[c, half_of(q), :]], axis=0)
        tok, sc = both[:, :WIDTH], both[:, WIDTH:]
        for k, mat in enumerate((wg, wu, wd)):
            for n0, nw in DOT_COLUMNS:
                cols = slice(n0, n0 + nw)
                if k < 2:
                    part = jnp.dot(tok, mat[:, cols], preferred_element_type=F32)
                else:
                    part = lax.dot_general(
                        sc, mat[cols, :], (((1,), (1,)), ((), ())), preferred_element_type=F32
                    )
                cs[r % 2, k, :, cols] = part[:HALF]
                acc[r % 5, k, :, cols] = part[HALF:]
            m_core(r, k).start()

    def forward_tokens():
        tok_msg(MATE, gat.at[OWN], core).wait_recv()
        for s in (2, 3):
            tok_msg(s, gat.at[MATE], tdev(-offsets[s][0] % 4, 0)).start()

    def send_far_tokens():
        tok_msg(4, gat.at[MATE], tdev(2, 0)).start()
        tok_msg(6, gat.at[OWN], tdev(2, 0)).start()

    def b_stage(c, r):
        a = r % 5
        for k in range(3):
            m_core(r, k).wait_recv()
        acc[a] += cr[r % 2]
        x1s[r % DEPTH] = acc[a, :, seg_of(xo), :CA].astype(BF16)
        m_x1p(r).start()
        m_x1m(r).start()
        y0s[r % DEPTH] = acc[a, :, :, mate_b].astype(BF16)
        m_y0(r).start()
        for k in range(3):
            m_core(r, k).wait_send()

    def c_stage(c, r):
        a = r % 5
        m_x1p(r).wait_recv()
        m_x1m(r).wait_recv()
        acc[a, :, seg_of(xp), :OA] += x1a[r % DEPTH].astype(F32)
        acc[a, :, seg_of(xm), OA:CA] += x1b[r % DEPTH].astype(F32)
        x2s[r % DEPTH, 0] = acc[a, :, seg_of(xp), :CA].astype(BF16)
        x2s[r % DEPTH, 1] = acc[a, :, seg_of(xm), :CA].astype(BF16)
        m_x2p(r).start()
        m_x2m(r).start()

    def c2_stage(c, r):
        a = r % 5
        m_y0(r).wait_recv()
        acc[a, :, :, own_b] += y0r[r % DEPTH].astype(F32)
        y1s[r % DEPTH] = acc[a, :, seg_of(xo), own_b].astype(BF16)
        m_y1p(r).start()
        m_y1m(r).start()

    def d_stage(c, r):
        a = r % 5
        m_x2p(r).wait_recv()
        m_x2m(r).wait_recv()
        acc[a, :, seg_of(x), :CA] += x2r[r % DEPTH, 0].astype(F32) + x2r[r % DEPTH, 1].astype(F32)
        zs[r % DEPTH] = acc[a, :, seg_of(x), mate_a].astype(BF16)
        m_zred(r).start()

    def d2_stage(c, r):
        a = r % 5
        m_y1p(r).wait_recv()
        m_y1m(r).wait_recv()
        acc[a, :, seg_of(xp), own_b_left] += y1a[r % DEPTH].astype(F32)
        acc[a, :, seg_of(xm), own_b_right] += y1b[r % DEPTH].astype(F32)
        y2s[r % DEPTH, 0] = acc[a, :, seg_of(xp), own_b].astype(BF16)
        y2s[r % DEPTH, 1] = acc[a, :, seg_of(xm), own_b].astype(BF16)
        m_y2p(r).start()
        m_y2m(r).start()

    def finish_units(c, tot, cols):
        gate, up, dhid = tot[0], tot[1], tot[2]
        sig = jax.nn.sigmoid(gate)
        hh[c, 0, rows_of(x), cols] = (gate * sig * up).astype(BF16)
        hh[c, 1, rows_of(x), cols] = (dhid * up * sig * (1.0 + gate * (1.0 - sig))).astype(BF16)
        hh[c, 2, rows_of(x), cols] = (dhid * gate * sig).astype(BF16)

    def e_stage(c, r):
        a = r % 5
        for message in (m_x1p(r), m_x1m(r), m_x2p(r), m_x2m(r), m_zred(r)):
            message.wait_send()
        m_zred(r).wait_recv()
        finish_units(c, acc[a, :, seg_of(x), own_a] + zr[r % DEPTH].astype(F32), own_a)
        m_zgat(c, out_a).start()

    def e2_stage(c, r):
        a = r % 5
        for message in (m_y0(r), m_y1p(r), m_y1m(r), m_y2p(r), m_y2m(r)):
            message.wait_send()
        m_y2p(r).wait_recv()
        m_y2m(r).wait_recv()
        tot = acc[a, :, seg_of(x), own_b] + y2r[r % DEPTH, 0].astype(F32) + y2r[r % DEPTH, 1].astype(F32)
        finish_units(c, tot, own_b)
        m_k1p(c, x).start()
        m_k1m(c, x).start()

    def f_stage(c):
        m_zgat(c, in_a).wait_recv()
        m_g1p(c, x).start()
        m_g1m(c, x).start()

    def f2_stage(c):
        m_k1p(c, xm).wait_recv()
        m_k2p(c, xm).start()
        m_k1m(c, xp).wait_recv()
        m_k2m(c, xp).start()

    def g_stage(c):
        m_g1p(c, xm).wait_recv()
        m_g2p(c, xm).start()
        m_g1m(c, xp).wait_recv()
        m_g2m(c, xp).start()

    def g2_stage(c):
        m_k2p(c, xo).wait_recv()
        m_k2m(c, xo).wait_recv()
        m_k3(c, out_b).start()

    def h_stage(c):
        m_g2p(c, xo).wait_recv()
        m_g2m(c, xo).wait_recv()
        m_k3(c, in_b).wait_recv()
        m_cgat(c, q).start()

    def i_stage(c):
        m_cgat(c, 1 - q).wait_recv()
        part = jnp.dot(hh[c, 0], wd[...], preferred_element_type=F32)

        @pl.when(c == OWN)
        def _():
            mown[...] = part

        @pl.when(c == MATE)
        def _():
            mfar[...] = part

        @pl.when((c != OWN) & (c != MATE))
        def _():
            ms[c] = part.astype(BF16)
            m_mix(c).start()

        tokens_c = cols_of(c * ROWS, ROWS)
        hidt[:, tokens_c] = hh[c, 0].T
        tokt[:, tokens_c] = gat[c, :, :WIDTH].T

    def join_mixed():
        for c in (2, 3, 4):
            m_mix(c).wait_recv()
            mfar[...] += mr[c].astype(F32)
        m_far().start()

    def early_gradient(k):
        depth = EARLY * ROWS
        for n0, nw in DOT_COLUMNS:
            block = pl.ds(n0, nw)
            right = hh[:EARLY, k + 1, :, block].reshape(depth, nw)
            early[k, :, block] = jnp.dot(tokt[:, :depth], right, preferred_element_type=F32)

    plan = [
        (e_stage, 5, False), (c_stage, 2, False), (g2_stage, 9, True), (g_stage, 11, True),
        (f_stage, 9, True), (b_stage, 1, False), (d_stage, 3, False), (f2_stage, 7, True),
        (a_partials, 0, False), (h_stage, 12, True), (e2_stage, 4, False), (c2_stage, 2, False),
        (d2_stage, 3, False), (i_stage, 13, True),
    ]
    last = max(lag for _, lag, _ in plan)

    def step(i, carry):
        for stage, lag, back in plan:
            j = i - lag
            @pl.when((j >= 0) & (j < SLOTS))
            def _(stage=stage, j=j, back=back):
                if back:
                    stage(j)
                else:
                    slot = jnp.where(j == 0, OWN, jnp.where(j == 1, 0, jnp.where(j == 2, 5, j - 2)))
                    stage(jnp.where(j == 7, 6, slot), j)

        @pl.when(i == 1)
        def _():
            forward_tokens()

        @pl.when(i == 2)
        def _():
            send_far_tokens()

        @pl.when(i == JOIN)
        def _():
            join_mixed()

        for k, at in enumerate(EARLY_STEPS):

            @pl.when(i == at)
            def _(k=k):
                early_gradient(k)

        return carry

    lax.fori_loop(0, SLOTS + last, step, 0)

    for c in (0, 5, 6):
        m_mix(c).wait_recv()
        mown[...] += mr[c].astype(F32)
    m_far().wait_recv()
    mown[...] += mfr[...]

    def drain(c, carry):
        for message in (
            m_zgat(c, out_a), m_g1p(c, x), m_g1m(c, x), m_g2p(c, xm), m_g2m(c, xp),
            m_cgat(c, q), m_k1p(c, x), m_k1m(c, x), m_k2p(c, xm), m_k2m(c, xp), m_k3(c, out_b),
        ):
            message.wait_send()

        @pl.when((c != OWN) & (c != MATE))
        def _():
            m_mix(c).wait_send()

        @pl.when(c != OWN)
        def _():
            tok_msg(c, gat.at[OWN], core).wait_send()

        return carry

    lax.fori_loop(0, SLOTS, drain, 0)
    m_far().wait_send()


def exchange(ids, tokens, grad_out, wg, wu, wd):
    vmem = pl.BlockSpec(memory_space=pltpu.VMEM)
    hbm = pl.BlockSpec(memory_space=pltpu.HBM)
    total = SLOTS * ROWS
    kinds = len(NAMES)
    return pl.pallas_call(
        exchange_kernel,
        name="exchange",
        out_shape=(
            pltpu.VMEM((ROWS, WIDTH), F32),
            pltpu.VMEM((SLOTS, ROWS, 2 * WIDTH), BF16),
            pltpu.VMEM((WIDTH, total), BF16),
            pltpu.VMEM((UNITS, total), BF16),
            pltpu.VMEM((SLOTS, 3, ROWS, UNITS), BF16),
            pltpu.VMEM((len(EARLY_STEPS), WIDTH, UNITS), F32),
        ),
        in_specs=[hbm] * 6,
        out_specs=(vmem,) * 6,
        scratch_shapes=[
            pltpu.VMEM((SLOTS, ROWS), jnp.int32),
            pltpu.VMEM((ROWS, WIDTH), BF16),
            pltpu.VMEM((WIDTH, UNITS), BF16),
            pltpu.VMEM((WIDTH, UNITS), BF16),
            pltpu.VMEM((UNITS, WIDTH), BF16),
            pltpu.VMEM((5, 3, HALF, UNITS), F32),
            pltpu.VMEM((2, 3, HALF, UNITS), F32),
            pltpu.VMEM((2, 3, HALF, UNITS), F32),
            pltpu.VMEM((DEPTH, 3, SEG, CA), BF16),
            pltpu.VMEM((DEPTH, 3, SEG, OA), BF16),
            pltpu.VMEM((DEPTH, 3, SEG, KA), BF16),
            pltpu.VMEM((DEPTH, 2, 3, SEG, CA), BF16),
            pltpu.VMEM((DEPTH, 2, 3, SEG, CA), BF16),
            pltpu.VMEM((DEPTH, 3, SEG, OA), BF16),
            pltpu.VMEM((DEPTH, 3, SEG, OA), BF16),
            pltpu.VMEM((DEPTH, 3, HALF, OB), BF16),
            pltpu.VMEM((DEPTH, 3, HALF, OB), BF16),
            pltpu.VMEM((DEPTH, 3, SEG, OB), BF16),
            pltpu.VMEM((DEPTH, 3, SEG, OL), BF16),
            pltpu.VMEM((DEPTH, 3, SEG, OR), BF16),
            pltpu.VMEM((DEPTH, 2, 3, SEG, OB), BF16),
            pltpu.VMEM((DEPTH, 2, 3, SEG, OB), BF16),
            pltpu.VMEM((OWN, ROWS, WIDTH), BF16),
            pltpu.VMEM((OWN, ROWS, WIDTH), BF16),
            pltpu.VMEM((ROWS, WIDTH), F32),
            pltpu.VMEM((ROWS, WIDTH), F32),
            pltpu.SemaphoreType.DMA((kinds, SLOTS)),
            pltpu.SemaphoreType.DMA((kinds, SLOTS)),
            pltpu.SemaphoreType.DMA((SLOTS,)),
            pltpu.SemaphoreType.DMA((SLOTS,)),
            pltpu.SemaphoreType.DMA((3,)),
            pltpu.SemaphoreType.DMA((3,)),
        ],
        compiler_params=pltpu.CompilerParams(
            collective_id=0, has_side_effects=True, vmem_limit_bytes=30 * 2**20
        ),
        cost_estimate=pl.CostEstimate(
            flops=8 * total * WIDTH * UNITS, bytes_accessed=24 * 2**20, transcendentals=0
        ),
    )(ids, tokens, grad_out, wg, wu, wd)


GRAD_COLUMNS = 640


def grads_kernel(
    mown, gat, tokt, hidt, hh, early,
    mixed, grad_gate, grad_up, grad_down,
    mbuf, gbuf, ubuf, dbuf, sems, msem,
):
    mbuf[...] = mown[...].astype(BF16)
    mcopy = pltpu.make_async_copy(mbuf, mixed, msem)
    mcopy.start()
    total = SLOTS * ROWS
    sc = gat[:, :, WIDTH:].reshape(total, WIDTH)
    blocks = []
    for n in range(UNITS // GRAD_COLUMNS):
        cols = pl.ds(n * GRAD_COLUMNS, GRAD_COLUMNS)
        slot = n % 2
        copies = [
            pltpu.make_async_copy(gbuf.at[slot], grad_gate.at[:, cols], sems.at[0, slot]),
            pltpu.make_async_copy(ubuf.at[slot], grad_up.at[:, cols], sems.at[1, slot]),
            pltpu.make_async_copy(dbuf.at[slot], grad_down.at[cols, :], sems.at[2, slot]),
        ]
        blocks.append(copies)
        for k, buf in enumerate((gbuf, ubuf, dbuf)):
            if n >= 2:
                blocks[n - 2][k].wait()
            if k < 2:
                first = EARLY if k < len(EARLY_STEPS) else 0
                depth = total - first * ROWS
                right = hh[first:, k + 1, :, cols].reshape(depth, GRAD_COLUMNS)
                part = jnp.dot(tokt[:, first * ROWS :], right, preferred_element_type=F32)
                buf[slot] = part + early[k, :, cols] if first else part
            else:
                buf[slot] = jnp.dot(hidt[cols, :], sc, preferred_element_type=F32)
            copies[k].start()
    for copies in blocks[-2:]:
        for copy in copies:
            copy.wait()
    mcopy.wait()


def grads(*arrays):
    total = SLOTS * ROWS
    vmem = pl.BlockSpec(memory_space=pltpu.VMEM)
    hbm = pl.BlockSpec(memory_space=pl.ANY)
    return pl.pallas_call(
        grads_kernel,
        name="grads",
        out_shape=(
            jax.ShapeDtypeStruct((ROWS, WIDTH), BF16),
            jax.ShapeDtypeStruct((WIDTH, UNITS), F32),
            jax.ShapeDtypeStruct((WIDTH, UNITS), F32),
            jax.ShapeDtypeStruct((UNITS, WIDTH), F32),
        ),
        in_specs=[vmem] * 6,
        out_specs=(hbm,) * 4,
        scratch_shapes=[
            pltpu.VMEM((ROWS, WIDTH), BF16),
            pltpu.VMEM((2, WIDTH, GRAD_COLUMNS), F32),
            pltpu.VMEM((2, WIDTH, GRAD_COLUMNS), F32),
            pltpu.VMEM((2, GRAD_COLUMNS, WIDTH), F32),
            pltpu.SemaphoreType.DMA((3, 2)),
            pltpu.SemaphoreType.DMA,
        ],
        compiler_params=pltpu.CompilerParams(vmem_limit_bytes=9 * 2**20),
        cost_estimate=pl.CostEstimate(
            flops=6 * total * WIDTH * UNITS, bytes_accessed=12 * 2**20, transcendentals=0
        ),
    )(*arrays)


def shards(tokens, segment_ids, gate_weight, up_weight, down_weight, grad_out):
    ids = segment_ids.reshape(SLOTS, ROWS)
    arrays = (ids, tokens, grad_out, gate_weight, up_weight, down_weight)
    outs = exchange(*(pltpu.with_memory_space_constraint(a, pltpu.HBM) for a in arrays))
    return grads(*outs)


def solution(mesh):
    placed = (
        P("tensor", "dp"),
        P(),
        P("dp", "tensor"),
        P("dp", "tensor"),
        P("tensor", "dp"),
        P("tensor", "dp"),
    )
    return jax.shard_map(
        shards,
        mesh=mesh,
        in_specs=placed,
        out_specs=(P("tensor", "dp"), P("dp", "tensor"), P("dp", "tensor"), P("tensor", "dp")),
        check_vma=False,
    )
```

profile of v0, /device:TPU:8, one launch (start us, length us, event | category | flops | bytes accessed | tf_op | source)
XLA Modules:
  0.0 116.7 jit_solution(6922421057041669719)
XLA Ops:
  0.6 109.5 %exchange.1 = (f32[128,512]{1,0:T(8,128)S(1)}, bf16[8,128,1024]{2,1,0:T(8,128)(2,1)S(1)}, bf16[512,1024]{1,0:T(8,128)(2,1)S(1)}, bf16[1920,1024]{1,0:T(8,128)(2,...) custom-call(s32[8,128]{1,0:T(8,128)} %bitcast.1, bf16[128,512]{1,0:T(8,128)(2,1)} %tokens_hbm.1, ...), custom_call_target="tpu_custom_call" | custom-call | flops 8053063680 | bytes 25165824 | tf_op jit(solution)/shard_map/exchange/pallas_call | solution.py:460
  110.2 6.5 %grads.1 = (bf16[128,512]{1,0:T(8,128)(2,1)}, f32[512,1920]{1,0:T(8,128)}, f32[512,1920]{1,0:T(8,128)}, f32[1920,512]{1,0:T(8,128)}) custom-call(f32[128,512]{1,0:T(8,128)S(1)} %get-tuple-element.10.mown, bf16[8,128,1024]{2,1,0:T(8,128)(2,1)S(1)} %get-tuple-element.11.gat, bf16[512,1024]{1,0:T(8,128)(2,1)S(1)} %get-tuple-element.12.tokt, ...), custom_call_target="tpu_custom_call" | custom-call | flops 6039797760 | bytes 12582912 | tf_op jit(solution)/shard_map/grads/pallas_call | solution.py:561
where the time goes:
time: 117 us
  Pallas kernels  116 us (99%)
    pallas_call x1, Pallas kernels, exchange(): pl.pallas_call(exchange_kernel, name='exchange', out_shape=(pltpu.VMEM((R...  110 us
    pallas_call x1, Pallas kernels, grads(): pl.pallas_call(grads_kernel, name='grads', out_shape=(jax.ShapeDtypeStruc...  6.52 us

commit v1 on v0

--- a/solution.py
+++ b/solution.py
@@ -352,6 +352,11 @@
 
     def i_stage(c):
         m_cgat(c, 1 - q).wait_recv()
+        for message in (
+            m_zgat(c, out_a), m_g1p(c, x), m_g1m(c, x), m_g2p(c, xm), m_g2m(c, xp),
+            m_cgat(c, q), m_k1p(c, x), m_k1m(c, x), m_k2p(c, xm), m_k2m(c, xp), m_k3(c, out_b),
+        ):
+            message.wait_send()
         part = jnp.dot(hh[c, 0], wd[...], preferred_element_type=F32)
 
         @pl.when(c == OWN)
@@ -432,12 +437,6 @@
     mown[...] += mfr[...]
 
     def drain(c, carry):
-        for message in (
-            m_zgat(c, out_a), m_g1p(c, x), m_g1m(c, x), m_g2p(c, xm), m_g2m(c, xp),
-            m_cgat(c, q), m_k1p(c, x), m_k1m(c, x), m_k2p(c, xm), m_k2m(c, xp), m_k3(c, out_b),
-        ):
-            message.wait_send()
-
         @pl.when((c != OWN) & (c != MATE))
         def _():
             m_mix(c).wait_send()

time: 117 us -> 117 us (level)
  no operation moved by 1% of the time
where the time goes in v1:
time: 117 us
  Pallas kernels  116 us (99%)
    pallas_call x1, Pallas kernels, exchange(): pl.pallas_call(exchange_kernel, name='exchange', out_shape=(pltpu.VMEM((R...  109 us
    pallas_call x1, Pallas kernels, grads(): pl.pallas_call(grads_kernel, name='grads', out_shape=(jax.ShapeDtypeStruc...  6.52 us

profile of v1, /device:TPU:8, one launch (start us, length us, event | category | flops | bytes accessed | tf_op | source)
XLA Modules:
  0.0 116.6 jit_solution(2354569552960539616)
XLA Ops:
  0.6 109.5 %exchange.1 = (f32[128,512]{1,0:T(8,128)S(1)}, bf16[8,128,1024]{2,1,0:T(8,128)(2,1)S(1)}, bf16[512,1024]{1,0:T(8,128)(2,1)S(1)}, bf16[1920,1024]{1,0:T(8,128)(2,...) custom-call(s32[8,128]{1,0:T(8,128)} %bitcast.1, bf16[128,512]{1,0:T(8,128)(2,1)} %tokens_hbm.1, ...), custom_call_target="tpu_custom_call" | custom-call | flops 8053063680 | bytes 25165824 | tf_op jit(solution)/shard_map/exchange/pallas_call | solution.py:459
  110.1 6.5 %grads.1 = (bf16[128,512]{1,0:T(8,128)(2,1)}, f32[512,1920]{1,0:T(8,128)}, f32[512,1920]{1,0:T(8,128)}, f32[1920,512]{1,0:T(8,128)}) custom-call(f32[128,512]{1,0:T(8,128)S(1)} %get-tuple-element.10.mown, bf16[8,128,1024]{2,1,0:T(8,128)(2,1)S(1)} %get-tuple-element.11.gat, bf16[512,1024]{1,0:T(8,128)(2,1)S(1)} %get-tuple-element.12.tokt, ...), custom_call_target="tpu_custom_call" | custom-call | flops 6039797760 | bytes 12582912 | tf_op jit(solution)/shard_map/grads/pallas_call | solution.py:560
